TPU v7x, 32 devices: a whole 2x2x4 slice. The times are simulated.
32 devices in a mesh: grp: 4 (over x, core), sub: 8 (over z, y).
Axes of the slice: x: 2, y: 2, z: 4, core: 2. Of those that a mesh axis runs over, the one named last changes fastest.
Arguments:
- right_side: float32 [65536, 128], P(('grp', 'sub')), may hold values from -6 to 6
- fine_values: float32 [81, 65536], P(None, ('grp', 'sub')), as said below
- columns: int32 [81, 65536], P(None, ('grp', 'sub')), may hold values from 0 to 2175, as said below
- agg_map: int32 [65536], P(('grp', 'sub')), may hold values from 0 to 127
- send_lo: int32 [2048], P(('grp', 'sub')), may hold values from 0 to 2047
- send_hi: int32 [2048], P(('grp', 'sub')), may hold values from 0 to 2047
- coarse_matrix: float32 [4, 1024, 1024], P('grp', 'sub'), as said below
Outputs:
- solution: float32 [65536, 128], P(('grp', 'sub'))
- residual: float32 [65536, 128], P(('grp', 'sub'))
Inputs may be any that keep to these rules, and one draw needn't show every extreme that they name: `columns`: entry 0 of row i of a partition is 64 + i, the others lie within 64 positions of it. `fine_values`: entry 0 lies in 2.5 to 5 and every other entry's magnitude is at most 0.06. `coarse_matrix`: symmetric; the diagonal lies in 10 to 20, other entries' magnitudes are at most 7.1 / sqrt(1024).
All inputs are finite; a program needn't handle non-finite values.
Results may differ from a plain program's by a relative error of at most 0.0001.
Values sent between devices are 32-bit elements; how exact they have to be, the bound alone decides.
A program may use at most 128 MiB of HBM per device.

v0:
```python
import jax
import jax.numpy as jnp
from jax import lax
from jax.sharding import PartitionSpec as P

CHEB_FINE = 2
CHEB_COARSE = 6
CYCLES = 2
THETA = 1.0
DELTA = 0.7
OMEGA = 0.6
highest = lax.Precision.HIGHEST


def from_behind(shard, axis, by):
    peers = lax.axis_size(axis)
    pairs = [(i, i + by) for i in range(peers) if 0 <= i + by < peers]
    return lax.ppermute(shard, axis, pairs)


def band_tiles(fine_values, columns, block_rows):
    rows_dev = columns.shape[1]
    rows = jnp.arange(rows_dev, dtype=jnp.int32)
    starts = rows // block_rows * block_rows
    local = columns - starts[None, :]
    places = jnp.arange(2 * block_rows, dtype=jnp.int32)[None, :]
    tiles = jnp.zeros((rows_dev, 2 * block_rows), jnp.float32)
    for entry in range(columns.shape[0]):
        tiles = tiles + jnp.where(local[entry][:, None] == places, fine_values[entry][:, None], 0.0)
    tiles = tiles.reshape(rows_dev // block_rows, block_rows, 2 * block_rows)
    return (tiles[:, :, :block_rows], tiles[:, :, block_rows:])


def selector(indices, count):
    return (indices[:, None] == jnp.arange(count, dtype=jnp.int32)[None, :]).astype(jnp.float32)


def fine_apply(vector, low_tiles, high_tiles, pick_lo, pick_hi):
    upper_rows = jnp.dot(pick_hi, vector, precision=highest)
    lower_rows = jnp.dot(pick_lo, vector, precision=highest)
    below = from_behind(upper_rows, ("grp", "sub"), 1)
    above = from_behind(lower_rows, ("grp", "sub"), -1)
    extended = jnp.concatenate([below, vector, above], 0)
    block_rows = low_tiles.shape[1]
    pieces = extended.reshape(-1, block_rows, vector.shape[1])
    total = jnp.einsum("brc,bcn->brn", low_tiles, pieces[:-1], precision=highest)
    total = total + jnp.einsum("brc,bcn->brn", high_tiles, pieces[1:], precision=highest)
    return total.reshape(vector.shape)


def chebyshev(residual, apply, inverse, steps, final):
    rho_old = DELTA / THETA
    direction = inverse * residual / THETA
    result = direction
    for turn in range(1, steps):
        residual = residual - apply(direction)
        rho_new = 1.0 / (2.0 * THETA / DELTA - rho_old)
        direction = rho_new * rho_old * direction + 2.0 * rho_new / DELTA * inverse * residual
        result = result + direction
        rho_old = rho_new
    if final:
        residual = residual - apply(direction)
    return (result, residual)


def body(right_side, fine_values, columns, agg_map, send_lo, send_hi, coarse_matrix):
    rows_dev = right_side.shape[0]
    low_tiles, high_tiles = band_tiles(fine_values, columns, 2 * send_lo.shape[0])
    pick_lo = selector(send_lo, rows_dev)
    pick_hi = selector(send_hi, rows_dev)

    def apply_fine(vector):
        return fine_apply(vector, low_tiles, high_tiles, pick_lo, pick_hi)

    own_rows = coarse_matrix[0]
    aggregates = own_rows.shape[0]
    sub_index = lax.axis_index("sub")
    start = sub_index * aggregates
    block = lax.dynamic_slice_in_dim(own_rows, start, aggregates, 1)
    coarse_inverse = 1.0 / jnp.diagonal(block)[:, None]

    def apply_coarse(vector):
        whole = lax.all_gather(vector, "sub", axis=0, tiled=True)
        return jnp.dot(own_rows, whole, precision=highest)

    dinv = 1.0 / fine_values[0][:, None]
    onehot = selector(agg_map, aggregates)
    solution = jnp.zeros_like(right_side)
    residual = right_side
    for cycle in range(CYCLES):
        update, residual = chebyshev(residual, apply_fine, dinv, CHEB_FINE, True)
        solution = solution + update
        smoothed = residual - OMEGA * apply_fine(dinv * residual)
        coarse_rhs = jnp.einsum("ra,rn->an", onehot, smoothed, precision=highest)
        result, unused = chebyshev(coarse_rhs, apply_coarse, coarse_inverse, CHEB_COARSE, False)
        spread = jnp.dot(onehot, result, precision=highest)
        correction = spread - OMEGA * dinv * apply_fine(spread)
        solution = solution + correction
        residual = residual - apply_fine(correction)
        update, residual = chebyshev(residual, apply_fine, dinv, CHEB_FINE, True)
        solution = solution + update
    return (solution, residual)


def solution(mesh):
    placed = (
        P(("grp", "sub"), None),
        P(None, ("grp", "sub")),
        P(None, ("grp", "sub")),
        P(("grp", "sub")),
        P(("grp", "sub")),
        P(("grp", "sub")),
        P("grp", "sub", None),
    )
    return jax.shard_map(
        body,
        mesh=mesh,
        in_specs=placed,
        out_specs=(P(("grp", "sub"), None), P(("grp", "sub"), None)),
        check_vma=False,
    )
```

profile of v0, /device:TPU:29, one launch (start us, length us, event | category | flops | bytes accessed | tf_op | source)
XLA Modules:
  0.0 596.2 jit_solution(620123093191027239)
XLA Ops:
  2.4 2.5 fusion.51
  4.9 2.1 collective-permute-start.1
  7.0 2.5 fusion.65
  9.6 7.1 %collective-permute-start = (f32[64,128]{1,0:T(8,128)}, f32[64,128]{1,0:T(8,128)S(1)}, u32[]{:S(2)}, u32[]{:S(2)}) collective-permute-start(f32[64,128]{1,0:T(8,128)} %fusion.65), channel_id=1, source_target_pairs={{0,1},{1,2},{2,3},{3,4},{4,5},{5,6},{6,7},{7,8},{8,9},{9,10},{10,1... | collective-permute-start | bytes 98312 | tf_op jit(solution)/shard_map/ppermute | solution.py:18
  21.6 47.7 %select_add_fusion = f32[16,128,256]{2,1,0:T(8,128)S(1)} fusion(f32[16,128]{1,0:T(8,128)S(1)} %bitcast.486, s32[16,128]{1,0:T(8,128)} %bitcast.608, f32[16,128]{1,0:T(8,128)S(1)} %bitcast.487, s32[16,128]{1,0:T(8,128)} %bitcast.609, f32[16,128]{1,0:T(8,128)S(1)} %bitcast.465, s32[16,128]{1,0:T(8,128)} %bitcast.610, f32[16,128]{1,0:T(8,128)S(1)} %bitcast.466, ...), kind=kLoop, calls=%fused_computation.1 | loop fusion | flops 126877696 | bytes 3424256 | tf_op jit(solution)/shard_map/add | solution.py:29
  76.7 1.9 collective-permute-start.2
  78.7 3.4 collective-permute-start.3
  82.1 5.4 collective-permute-done.3
  91.7 1.9 collective-permute-start.4
  93.6 3.6 collective-permute-start.5
  97.2 5.2 collective-permute-done.5
  107.1 26.0 %all_gather.30 = f32[1024,128]{1,0:T(8,128)S(1)} all-gather(f32[128,128]{1,0:T(8,128)S(1)} %get-tuple-element.209), channel_id=1, replica_groups=mesh['grp'=4,'sub'=8] {'sub'}, dimensions={0}, use_global_device_ids=true | all-gather | bytes 589824 | tf_op jit(solution)/shard_map/all_gather | solution.py:83
  133.8 25.7 %all_gather.31 = f32[1024,128]{1,0:T(8,128)S(1)} all-gather(f32[128,128]{1,0:T(8,128)S(1)} %get-tuple-element.211), channel_id=1, replica_groups=mesh['grp'=4,'sub'=8] {'sub'}, dimensions={0}, use_global_device_ids=true | all-gather | bytes 589824 | tf_op jit(solution)/shard_map/all_gather | solution.py:83
  160.1 25.7 %all_gather.32 = f32[1024,128]{1,0:T(8,128)S(1)} all-gather(f32[128,128]{1,0:T(8,128)S(1)} %get-tuple-element.213), channel_id=1, replica_groups=mesh['grp'=4,'sub'=8] {'sub'}, dimensions={0}, use_global_device_ids=true | all-gather | bytes 589824 | tf_op jit(solution)/shard_map/all_gather | solution.py:83
  186.5 25.4 %all_gather.33 = f32[1024,128]{1,0:T(8,128)S(1)} all-gather(f32[128,128]{1,0:T(8,128)S(1)} %get-tuple-element.215), channel_id=1, replica_groups=mesh['grp'=4,'sub'=8] {'sub'}, dimensions={0}, use_global_device_ids=true | all-gather | bytes 589824 | tf_op jit(solution)/shard_map/all_gather | solution.py:83
  212.5 25.6 %all_gather.34 = f32[1024,128]{1,0:T(8,128)S(1)} all-gather(f32[128,128]{1,0:T(8,128)S(1)} %get-tuple-element.217), channel_id=1, replica_groups=mesh['grp'=4,'sub'=8] {'sub'}, dimensions={0}, use_global_device_ids=true | all-gather | bytes 589824 | tf_op jit(solution)/shard_map/all_gather | solution.py:83
  240.8 30.2 %collective-permute-start.6 = (f32[64,128]{1,0:T(8,128)S(1)}, f32[64,128]{1,0:T(8,128)S(1)}, u32[]{:S(2)}, u32[]{:S(2)}) collective-permute-start(f32[64,128]{1,0:T(8,128)S(1)} %fusion.62), channel_id=1, source_target_pairs={{0,1},{1,2},{2,3},{3,4},{4,5},{5,6},{6,7},{7,8},{8,9},{9,10},{10,1... | collective-permute-start | bytes 98312 | tf_op jit(solution)/shard_map/ppermute | solution.py:18
  271.0 2.2 collective-permute-start.7
  273.2 6.6 %collective-permute-done.7 = f32[64,128]{1,0:T(8,128)S(1)} collective-permute-done((f32[64,128]{1,0:T(8,128)S(1)}, f32[64,128]{1,0:T(8,128)S(1)}, u32[]{:S(2)}, u32[]{:S(2)}) %collective-permute-start.7) | collective-permute-done | bytes 32800 | tf_op jit(solution)/shard_map/ppermute | solution.py:18
  284.0 1.9 collective-permute-start.8
  285.9 3.4 collective-permute-start.9
  289.3 5.4 collective-permute-done.9
  298.8 1.9 collective-permute-start.10
  300.7 3.8 collective-permute-start.11
  304.5 5.0 collective-permute-done.11
  313.6 1.9 collective-permute-start.12
  315.5 3.4 collective-permute-start.13
  318.9 5.4 collective-permute-done.13
  330.3 3.5 collective-permute-start.15
  333.9 5.3 collective-permute-done.15
  345.2 3.4 collective-permute-start.17
  348.6 5.4 collective-permute-done.17
  360.0 3.6 collective-permute-start.19
  363.6 5.2 collective-permute-done.19
  373.0 24.9 %all_gather.35 = f32[1024,128]{1,0:T(8,128)S(1)} all-gather(f32[128,128]{1,0:T(8,128)S(1)} %get-tuple-element.219), channel_id=1, replica_groups=mesh['grp'=4,'sub'=8] {'sub'}, dimensions={0}, use_global_device_ids=true | all-gather | bytes 589824 | tf_op jit(solution)/shard_map/all_gather | solution.py:83
  398.5 25.4 %all_gather.36 = f32[1024,128]{1,0:T(8,128)S(1)} all-gather(f32[128,128]{1,0:T(8,128)S(1)} %get-tuple-element.221), channel_id=1, replica_groups=mesh['grp'=4,'sub'=8] {'sub'}, dimensions={0}, use_global_device_ids=true | all-gather | bytes 589824 | tf_op jit(solution)/shard_map/all_gather | solution.py:83
  424.6 26.1 %all_gather.37 = f32[1024,128]{1,0:T(8,128)S(1)} all-gather(f32[128,128]{1,0:T(8,128)S(1)} %get-tuple-element.223), channel_id=1, replica_groups=mesh['grp'=4,'sub'=8] {'sub'}, dimensions={0}, use_global_device_ids=true | all-gather | bytes 589824 | tf_op jit(solution)/shard_map/all_gather | solution.py:83
  451.3 25.9 %all_gather.38 = f32[1024,128]{1,0:T(8,128)S(1)} all-gather(f32[128,128]{1,0:T(8,128)S(1)} %get-tuple-element.225), channel_id=1, replica_groups=mesh['grp'=4,'sub'=8] {'sub'}, dimensions={0}, use_global_device_ids=true | all-gather | bytes 589824 | tf_op jit(solution)/shard_map/all_gather | solution.py:83
  477.8 25.3 %all_gather.39 = f32[1024,128]{1,0:T(8,128)S(1)} all-gather(f32[128,128]{1,0:T(8,128)S(1)} %get-tuple-element.227), channel_id=1, replica_groups=mesh['grp'=4,'sub'=8] {'sub'}, dimensions={0}, use_global_device_ids=true | all-gather | bytes 589824 | tf_op jit(solution)/shard_map/all_gather | solution.py:83
  505.8 31.2 %collective-permute-start.20 = (f32[64,128]{1,0:T(8,128)S(1)}, f32[64,128]{1,0:T(8,128)S(1)}, u32[]{:S(2)}, u32[]{:S(2)}) collective-permute-start(f32[64,128]{1,0:T(8,128)S(1)} %fusion.55), channel_id=1, source_target_pairs={{0,1},{1,2},{2,3},{3,4},{4,5},{5,6},{6,7},{7,8},{8,9},{9,10},{10,1... | collective-permute-start | bytes 98312 | tf_op jit(solution)/shard_map/ppermute | solution.py:18
  537.1 2.2 collective-permute-start.21
  539.3 6.6 %collective-permute-done.21 = f32[64,128]{1,0:T(8,128)S(1)} collective-permute-done((f32[64,128]{1,0:T(8,128)S(1)}, f32[64,128]{1,0:T(8,128)S(1)}, u32[]{:S(2)}, u32[]{:S(2)}) %collective-permute-start.21) | collective-permute-done | bytes 32800 | tf_op jit(solution)/shard_map/ppermute | solution.py:18
  551.9 3.4 collective-permute-start.23
  555.3 5.6 collective-permute-done.23
  566.9 3.7 collective-permute-start.25
  570.5 5.2 collective-permute-done.25
  583.1 3.4 collective-permute-start.27
  586.5 5.4 collective-permute-done.27
  (152 shorter events, 90.3 us)
Async XLA Ops:
  0.6 21.0 %copy-start = (f32[1,128,1024]{2,1,0:T(8,128)S(1)}, f32[1,128,1024]{2,1,0:T(8,128)}, u32[]{:S(2)}) copy-start(f32[1,128,1024]{2,1,0:T(8,128)} %param.13) | copy-start | bytes 1572868
  0.6 16.1 %copy-start.4 = (f32[81,2048]{1,0:T(8,128)S(1)}, f32[81,2048]{1,0:T(8,128)}, u32[]{:S(2)}) copy-start(f32[81,2048]{1,0:T(8,128)} %param.8) | copy-start | bytes 1990660
  0.7 16.5 %copy-start.3 = (s32[81,2048]{1,0:T(8,128)S(1)}, s32[81,2048]{1,0:T(8,128)}, u32[]{:S(2)}) copy-start(s32[81,2048]{1,0:T(8,128)} %param.9) | copy-start | bytes 1990660
  4.9 65.7 %collective-permute-start.1 = (f32[64,128]{1,0:T(8,128)}, f32[64,128]{1,0:T(8,128)S(1)}, u32[]{:S(2)}, u32[]{:S(2)}) collective-permute-start(f32[64,128]{1,0:T(8,128)} %fusion.51), channel_id=1, source_target_pairs={{1,0},{2,1},{3,2},{4,3},{5,4},{6,5},{7,6},{8,7},{9,8},{10,9},{11,1... | collective-permute-start | bytes 98312 | tf_op jit(solution)/shard_map/ppermute | solution.py:18
  9.6 10.7 %copy-start.1 = (f32[2048,128]{1,0:T(8,128)S(1)}, f32[2048,128]{1,0:T(8,128)}, u32[]{:S(2)}) copy-start(f32[2048,128]{1,0:T(8,128)} %param.7) | copy-start | bytes 3145732
  9.6 61.1 %collective-permute-start = (f32[64,128]{1,0:T(8,128)}, f32[64,128]{1,0:T(8,128)S(1)}, u32[]{:S(2)}, u32[]{:S(2)}) collective-permute-start(f32[64,128]{1,0:T(8,128)} %fusion.65), channel_id=1, source_target_pairs={{0,1},{1,2},{2,3},{3,4},{4,5},{5,6},{6,7},{7,8},{8,9},{9,10},{10,1... | collective-permute-start | bytes 98312 | tf_op jit(solution)/shard_map/ppermute | solution.py:18
  73.5 1.2 copy-start.2
  74.7 0.8 copy-start.6
  74.8 1.4 copy-start.7
  76.7 5.3 collective-permute-start.2
  78.7 8.8 %collective-permute-start.3 = (f32[64,128]{1,0:T(8,128)S(1)}, f32[64,128]{1,0:T(8,128)S(1)}, u32[]{:S(2)}, u32[]{:S(2)}) collective-permute-start(f32[64,128]{1,0:T(8,128)S(1)} %fusion.50), channel_id=1, source_target_pairs={{1,0},{2,1},{3,2},{4,3},{5,4},{6,5},{7,6},{8,7},{9,8},{10,9},{11,1... | collective-permute-start | bytes 98312 | tf_op jit(solution)/shard_map/ppermute | solution.py:18
  91.7 5.5 collective-permute-start.4
  93.6 8.8 %collective-permute-start.5 = (f32[64,128]{1,0:T(8,128)S(1)}, f32[64,128]{1,0:T(8,128)S(1)}, u32[]{:S(2)}, u32[]{:S(2)}) collective-permute-start(f32[64,128]{1,0:T(8,128)S(1)} %fusion.49), channel_id=1, source_target_pairs={{1,0},{2,1},{3,2},{4,3},{5,4},{6,5},{7,6},{8,7},{9,8},{10,9},{11,1... | collective-permute-start | bytes 98312 | tf_op jit(solution)/shard_map/ppermute | solution.py:18
  105.0 0.7 copy-start.5
  240.8 32.4 %collective-permute-start.6 = (f32[64,128]{1,0:T(8,128)S(1)}, f32[64,128]{1,0:T(8,128)S(1)}, u32[]{:S(2)}, u32[]{:S(2)}) collective-permute-start(f32[64,128]{1,0:T(8,128)S(1)} %fusion.62), channel_id=1, source_target_pairs={{0,1},{1,2},{2,3},{3,4},{4,5},{5,6},{6,7},{7,8},{8,9},{9,10},{10,1... | collective-permute-start | bytes 98312 | tf_op jit(solution)/shard_map/ppermute | solution.py:18
  271.0 8.8 %collective-permute-start.7 = (f32[64,128]{1,0:T(8,128)S(1)}, f32[64,128]{1,0:T(8,128)S(1)}, u32[]{:S(2)}, u32[]{:S(2)}) collective-permute-start(f32[64,128]{1,0:T(8,128)S(1)} %fusion.48), channel_id=1, source_target_pairs={{1,0},{2,1},{3,2},{4,3},{5,4},{6,5},{7,6},{8,7},{9,8},{10,9},{11,1... | collective-permute-start | bytes 98312 | tf_op jit(solution)/shard_map/ppermute | solution.py:18
  284.0 5.3 collective-permute-start.8
  285.9 8.8 %collective-permute-start.9 = (f32[64,128]{1,0:T(8,128)S(1)}, f32[64,128]{1,0:T(8,128)S(1)}, u32[]{:S(2)}, u32[]{:S(2)}) collective-permute-start(f32[64,128]{1,0:T(8,128)S(1)} %fusion.47), channel_id=1, source_target_pairs={{1,0},{2,1},{3,2},{4,3},{5,4},{6,5},{7,6},{8,7},{9,8},{10,9},{11,1... | collective-permute-start | bytes 98312 | tf_op jit(solution)/shard_map/ppermute | solution.py:18
  298.8 5.8 collective-permute-start.10
  300.7 8.8 %collective-permute-start.11 = (f32[64,128]{1,0:T(8,128)S(1)}, f32[64,128]{1,0:T(8,128)S(1)}, u32[]{:S(2)}, u32[]{:S(2)}) collective-permute-start(f32[64,128]{1,0:T(8,128)S(1)} %fusion.46), channel_id=1, source_target_pairs={{1,0},{2,1},{3,2},{4,3},{5,4},{6,5},{7,6},{8,7},{9,8},{10,9},{11,1... | collective-permute-start | bytes 98312 | tf_op jit(solution)/shard_map/ppermute | solution.py:18
  313.6 5.3 collective-permute-start.12
  315.5 8.8 %collective-permute-start.13 = (f32[64,128]{1,0:T(8,128)S(1)}, f32[64,128]{1,0:T(8,128)S(1)}, u32[]{:S(2)}, u32[]{:S(2)}) collective-permute-start(f32[64,128]{1,0:T(8,128)S(1)} %fusion.45), channel_id=1, source_target_pairs={{1,0},{2,1},{3,2},{4,3},{5,4},{6,5},{7,6},{8,7},{9,8},{10,9},{11,1... | collective-permute-start | bytes 98312 | tf_op jit(solution)/shard_map/ppermute | solution.py:18
  328.4 5.5 collective-permute-start.14
  330.3 8.8 %collective-permute-start.15 = (f32[64,128]{1,0:T(8,128)S(1)}, f32[64,128]{1,0:T(8,128)S(1)}, u32[]{:S(2)}, u32[]{:S(2)}) collective-permute-start(f32[64,128]{1,0:T(8,128)S(1)} %fusion.44), channel_id=1, source_target_pairs={{1,0},{2,1},{3,2},{4,3},{5,4},{6,5},{7,6},{8,7},{9,8},{10,9},{11,1... | collective-permute-start | bytes 98312 | tf_op jit(solution)/shard_map/ppermute | solution.py:18
  343.2 5.3 collective-permute-start.16
  345.2 8.8 %collective-permute-start.17 = (f32[64,128]{1,0:T(8,128)S(1)}, f32[64,128]{1,0:T(8,128)S(1)}, u32[]{:S(2)}, u32[]{:S(2)}) collective-permute-start(f32[64,128]{1,0:T(8,128)S(1)} %fusion.43), channel_id=1, source_target_pairs={{1,0},{2,1},{3,2},{4,3},{5,4},{6,5},{7,6},{8,7},{9,8},{10,9},{11,1... | collective-permute-start | bytes 98312 | tf_op jit(solution)/shard_map/ppermute | solution.py:18
  358.1 5.5 collective-permute-start.18
  360.0 8.8 %collective-permute-start.19 = (f32[64,128]{1,0:T(8,128)S(1)}, f32[64,128]{1,0:T(8,128)S(1)}, u32[]{:S(2)}, u32[]{:S(2)}) collective-permute-start(f32[64,128]{1,0:T(8,128)S(1)} %fusion.42), channel_id=1, source_target_pairs={{1,0},{2,1},{3,2},{4,3},{5,4},{6,5},{7,6},{8,7},{9,8},{10,9},{11,1... | collective-permute-start | bytes 98312 | tf_op jit(solution)/shard_map/ppermute | solution.py:18
  505.8 33.4 %collective-permute-start.20 = (f32[64,128]{1,0:T(8,128)S(1)}, f32[64,128]{1,0:T(8,128)S(1)}, u32[]{:S(2)}, u32[]{:S(2)}) collective-permute-start(f32[64,128]{1,0:T(8,128)S(1)} %fusion.55), channel_id=1, source_target_pairs={{0,1},{1,2},{2,3},{3,4},{4,5},{5,6},{6,7},{7,8},{8,9},{9,10},{10,1... | collective-permute-start | bytes 98312 | tf_op jit(solution)/shard_map/ppermute | solution.py:18
  537.1 8.8 %collective-permute-start.21 = (f32[64,128]{1,0:T(8,128)S(1)}, f32[64,128]{1,0:T(8,128)S(1)}, u32[]{:S(2)}, u32[]{:S(2)}) collective-permute-start(f32[64,128]{1,0:T(8,128)S(1)} %fusion.41), channel_id=1, source_target_pairs={{1,0},{2,1},{3,2},{4,3},{5,4},{6,5},{7,6},{8,7},{9,8},{10,9},{11,1... | collective-permute-start | bytes 98312 | tf_op jit(solution)/shard_map/ppermute | solution.py:18
  550.0 5.3 collective-permute-start.22
  551.9 8.9 %collective-permute-start.23 = (f32[64,128]{1,0:T(8,128)S(1)}, f32[64,128]{1,0:T(8,128)S(1)}, u32[]{:S(2)}, u32[]{:S(2)}) collective-permute-start(f32[64,128]{1,0:T(8,128)S(1)} %fusion.40), channel_id=1, source_target_pairs={{1,0},{2,1},{3,2},{4,3},{5,4},{6,5},{7,6},{8,7},{9,8},{10,9},{11,1... | collective-permute-start | bytes 98312 | tf_op jit(solution)/shard_map/ppermute | solution.py:18
  564.9 5.6 collective-permute-start.24
  566.9 8.8 %collective-permute-start.25 = (f32[64,128]{1,0:T(8,128)S(1)}, f32[64,128]{1,0:T(8,128)S(1)}, u32[]{:S(2)}, u32[]{:S(2)}) collective-permute-start(f32[64,128]{1,0:T(8,128)S(1)} %fusion.39), channel_id=1, source_target_pairs={{1,0},{2,1},{3,2},{4,3},{5,4},{6,5},{7,6},{8,7},{9,8},{10,9},{11,1... | collective-permute-start | bytes 98312 | tf_op jit(solution)/shard_map/ppermute | solution.py:18
  581.2 5.3 collective-permute-start.26
  583.1 8.8 %collective-permute-start.27 = (f32[64,128]{1,0:T(8,128)S(1)}, f32[64,128]{1,0:T(8,128)S(1)}, u32[]{:S(2)}, u32[]{:S(2)}) collective-permute-start(f32[64,128]{1,0:T(8,128)S(1)} %fusion.38), channel_id=1, source_target_pairs={{1,0},{2,1},{3,2},{4,3},{5,4},{6,5},{7,6},{8,7},{9,8},{10,9},{11,1... | collective-permute-start | bytes 98312 | tf_op jit(solution)/shard_map/ppermute | solution.py:18
where the time goes:
time: 600 us; the launch traced here: 596 us
  blocking collectives  256 us (43%)
  starting transfers between devices  135 us (22%)
  waiting for transfers between devices  72 us (12%)
  matrix products  64.9 us (11%)
  other arithmetic  61.3 us (10%)
    all_gather x10, blocking collectives, apply_coarse(): whole = lax.all_gather(vector, 'sub', axis=0, tiled=True)  256 us
    ppermute x28, starting transfers between devices, from_behind(): return lax.ppermute(shard, axis, pairs)  135 us
    ppermute x28, waiting for transfers between devices, from_behind(): return lax.ppermute(shard, axis, pairs)  72 us
    add x1, other arithmetic, band_tiles(): tiles + jnp.where(local[entry][:, None] == places, fine_values[entry][:,...  47.7 us
    dot_general x14, matrix products, fine_apply(): jnp.einsum('brc,bcn->brn', low_tiles, pieces[:-1], precision=highest)  17.3 us
    dot_general x14, matrix products, fine_apply(): jnp.einsum('brc,bcn->brn', high_tiles, pieces[1:], precision=highest)  16.8 us
  transfers between devices with their start and end apart: 28, of which 13 were waited for; matrix products, arithmetic and copies ran while one was open for 9% of the time, Pallas kernels for 0%

commit v1 on v0

--- a/solution.py
+++ b/solution.py
@@ -10,6 +10,19 @@
 DELTA = 0.7
 OMEGA = 0.6
 highest = lax.Precision.HIGHEST
+
+
+def collect(value, axis, dim):
+    ways = lax.axis_size(axis)
+    up = [(d, (d + 1) % ways) for d in range(ways)]
+    down = [(d, (d - 1) % ways) for d in range(ways)]
+    earlier, later = ([value], [value])
+    for _ in range(ways // 2):
+        earlier.append(lax.ppermute(earlier[-1], axis, up))
+    for _ in range((ways - 1) // 2):
+        later.append(lax.ppermute(later[-1], axis, down))
+    line = jnp.concatenate([*earlier[::-1], *later[1:]], axis=dim)
+    return jnp.roll(line, (lax.axis_index(axis) - ways // 2) * value.shape[dim], axis=dim)
 
 
 def from_behind(shard, axis, by):
@@ -80,7 +93,7 @@
     coarse_inverse = 1.0 / jnp.diagonal(block)[:, None]
 
     def apply_coarse(vector):
-        whole = lax.all_gather(vector, "sub", axis=0, tiled=True)
+        whole = collect(vector, "sub", 0)
         return jnp.dot(own_rows, whole, precision=highest)
 
     dinv = 1.0 / fine_values[0][:, None]

time: 600 us -> 572 us (0.953)
  blocking collectives: 256 us -> 0 us
  waiting for transfers between devices: 72 us -> 189 us
  starting transfers between devices: 135 us -> 240 us
    all_gather x10 -> x0, blocking collectives: 256 us -> none  [apply_coarse(): whole = lax.all_gather(vector, 'sub', axis=0, tiled=True)]
    ppermute x0 -> x70, starting transfers between devices: none -> 120 us  [the longest x40 120 us: collect(): earlier.append(lax.ppermute(earlier[-1], axis, up))]
    ppermute x0 -> x70, waiting for transfers between devices: none -> 118 us  [the longest x40 71.9 us: collect(): earlier.append(lax.ppermute(earlier[-1], axis, up))]
    ppermute x28, starting transfers between devices: 135 us -> 120 us  [from_behind(): return lax.ppermute(shard, axis, pairs)]
  transfers between devices with their start and end apart: 28 -> 98, of which waited for: 13 -> 69; matrix products, arithmetic and copies ran while one was open for 9% -> 10% of each run, Pallas kernels for 0% -> 0%
where the time goes in v1:
time: 572 us; the launch traced here: 568 us
  starting transfers between devices  240 us (42%)
  waiting for transfers between devices  189 us (33%)
  matrix products  66.9 us (12%)
  other arithmetic  61.8 us (11%)
  local copies, waits for them, and re-layouts  6.73 us (1%)
    ppermute x28, starting transfers between devices, from_behind(): return lax.ppermute(shard, axis, pairs)  120 us
    ppermute x40, starting transfers between devices, collect(): earlier.append(lax.ppermute(earlier[-1], axis, up))  120 us
    ppermute x40, waiting for transfers between devices, collect(): earlier.append(lax.ppermute(earlier[-1], axis, up))  71.9 us
    ppermute x28, waiting for transfers between devices, from_behind(): return lax.ppermute(shard, axis, pairs)  71 us
    add x1, other arithmetic, band_tiles(): tiles + jnp.where(local[entry][:, None] == places, fine_values[entry][:,...  46.7 us
    ppermute x30, waiting for transfers between devices, collect(): later.append(lax.ppermute(later[-1], axis, down))  46.4 us
    dot_general x14, matrix products, fine_apply(): jnp.einsum('brc,bcn->brn', low_tiles, pieces[:-1], precision=highest)  17.3 us
    dot_general x14, matrix products, fine_apply(): jnp.einsum('brc,bcn->brn', high_tiles, pieces[1:], precision=highest)  16.7 us
  transfers between devices with their start and end apart: 98, of which 69 were waited for; matrix products, arithmetic and copies ran while one was open for 10% of the time, Pallas kernels for 0%

profile of v1, /device:TPU:29, one launch (start us, length us, event | category | flops | bytes accessed | tf_op | source)
XLA Modules:
  0.0 567.9 jit_solution(3810402405419202775)
XLA Ops:
  9.5 7.1 %collective-permute-start = (f32[64,128]{1,0:T(8,128)}, f32[64,128]{1,0:T(8,128)S(1)}, u32[]{:S(2)}, u32[]{:S(2)}) collective-permute-start(f32[64,128]{1,0:T(8,128)} %fusion.85), channel_id=1, source_target_pairs={{0,1},{1,2},{2,3},{3,4},{4,5},{5,6},{6,7},{7,8},{8,9},{9,10},{10,1... | collective-permute-start | bytes 98312 | tf_op jit(solution)/shard_map/ppermute | solution.py:31
  21.5 46.7 %select_add_fusion = f32[16,128,256]{2,1,0:T(8,128)S(1)} fusion(f32[16,128]{1,0:T(8,128)S(1)} %bitcast.476, s32[16,128]{1,0:T(8,128)} %bitcast.598, f32[16,128]{1,0:T(8,128)S(1)} %bitcast.477, s32[16,128]{1,0:T(8,128)} %bitcast.599, f32[16,128]{1,0:T(8,128)S(1)} %bitcast.455, s32[16,128]{1,0:T(8,128)} %bitcast.600, f32[16,128]{1,0:T(8,128)S(1)} %bitcast.456, ...), kind=kLoop, calls=%fused_computation.1 | loop fusion | flops 126877696 | bytes 3424256 | tf_op jit(solution)/shard_map/add | solution.py:42
  81.4 4.2 collective-permute-done.3
  97.2 5.0 collective-permute-done.5
  114.1 4.5 collective-permute-start.8
  119.9 5.0 collective-permute-start.9
  126.4 4.4 collective-permute-done.12
  139.0 4.5 collective-permute-start.15
  144.8 4.5 collective-permute-start.16
  150.7 4.6 collective-permute-done.19
  163.4 4.5 collective-permute-start.22
  169.2 4.6 collective-permute-start.23
  175.2 4.4 collective-permute-done.26
  187.8 4.5 collective-permute-start.29
  194.0 4.9 collective-permute-start.30
  200.3 4.4 collective-permute-done.33
  212.9 4.6 collective-permute-start.36
  218.8 4.5 collective-permute-start.37
  224.7 4.6 collective-permute-done.40
  232.2 24.5 %collective-permute-start.41 = (f32[64,128]{1,0:T(8,128)S(1)}, f32[64,128]{1,0:T(8,128)S(1)}, u32[]{:S(2)}, u32[]{:S(2)}) collective-permute-start(f32[64,128]{1,0:T(8,128)S(1)} %fusion.82), channel_id=1, source_target_pairs={{0,1},{1,2},{2,3},{3,4},{4,5},{5,6},{6,7},{7,8},{8,9},{9,10},{10,1... | collective-permute-start | bytes 98312 | tf_op jit(solution)/shard_map/ppermute | solution.py:31
  258.7 6.9 %collective-permute-done.42 = f32[64,128]{1,0:T(8,128)S(1)} collective-permute-done((f32[64,128]{1,0:T(8,128)S(1)}, f32[64,128]{1,0:T(8,128)S(1)}, u32[]{:S(2)}, u32[]{:S(2)}) %collective-permute-start.42) | collective-permute-done | bytes 32800 | tf_op jit(solution)/shard_map/ppermute | solution.py:31
  274.9 5.4 collective-permute-done.44
  290.0 5.2 collective-permute-done.46
  304.6 5.4 collective-permute-done.48
  316.0 3.8 collective-permute-start.50
  319.8 5.0 collective-permute-done.50
  334.2 5.4 collective-permute-done.52
  349.3 5.3 collective-permute-done.54
  366.4 4.7 collective-permute-start.57
  372.4 4.5 collective-permute-start.58
  378.3 4.5 collective-permute-done.61
  390.9 4.5 collective-permute-start.64
  396.7 4.5 collective-permute-start.65
  402.9 5.2 collective-permute-done.68
  416.6 4.5 collective-permute-start.71
  422.4 4.6 collective-permute-start.72
  428.4 4.4 collective-permute-done.75
  441.0 4.5 collective-permute-start.78
  447.3 4.9 collective-permute-start.79
  453.7 4.4 collective-permute-done.82
  466.2 4.5 collective-permute-start.85
  472.1 4.5 collective-permute-start.86
  478.0 4.6 collective-permute-done.89
  485.6 23.3 %collective-permute-start.90 = (f32[64,128]{1,0:T(8,128)S(1)}, f32[64,128]{1,0:T(8,128)S(1)}, u32[]{:S(2)}, u32[]{:S(2)}) collective-permute-start(f32[64,128]{1,0:T(8,128)S(1)} %fusion.75), channel_id=1, source_target_pairs={{0,1},{1,2},{2,3},{3,4},{4,5},{5,6},{6,7},{7,8},{8,9},{9,10},{10,1... | collective-permute-start | bytes 98312 | tf_op jit(solution)/shard_map/ppermute | solution.py:31
  510.8 6.9 %collective-permute-done.91 = f32[64,128]{1,0:T(8,128)S(1)} collective-permute-done((f32[64,128]{1,0:T(8,128)S(1)}, f32[64,128]{1,0:T(8,128)S(1)}, u32[]{:S(2)}, u32[]{:S(2)}) %collective-permute-start.91) | collective-permute-done | bytes 32800 | tf_op jit(solution)/shard_map/ppermute | solution.py:31
  527.0 5.4 collective-permute-done.93
  542.1 5.2 collective-permute-done.95
  558.4 5.4 collective-permute-done.97
  (378 shorter events, 251.8 us)
Async XLA Ops:
  4.9 63.4 %collective-permute-start.1 = (f32[64,128]{1,0:T(8,128)}, f32[64,128]{1,0:T(8,128)S(1)}, u32[]{:S(2)}, u32[]{:S(2)}) collective-permute-start(f32[64,128]{1,0:T(8,128)} %fusion.71), channel_id=1, source_target_pairs={{1,0},{2,1},{3,2},{4,3},{5,4},{6,5},{7,6},{8,7},{9,8},{10,9},{11,1... | collective-permute-start | bytes 98312 | tf_op jit(solution)/shard_map/ppermute | solution.py:31
  9.5 58.8 %collective-permute-start = (f32[64,128]{1,0:T(8,128)}, f32[64,128]{1,0:T(8,128)S(1)}, u32[]{:S(2)}, u32[]{:S(2)}) collective-permute-start(f32[64,128]{1,0:T(8,128)} %fusion.85), channel_id=1, source_target_pairs={{0,1},{1,2},{2,3},{3,4},{4,5},{5,6},{6,7},{7,8},{8,9},{9,10},{10,1... | collective-permute-start | bytes 98312 | tf_op jit(solution)/shard_map/ppermute | solution.py:31
  74.8 6.6 %collective-permute-start.2 = (f32[64,128]{1,0:T(8,128)S(1)}, f32[64,128]{1,0:T(8,128)S(1)}, u32[]{:S(2)}, u32[]{:S(2)}) collective-permute-start(f32[64,128]{1,0:T(8,128)S(1)} %fusion.84), channel_id=1, source_target_pairs={{0,1},{1,2},{2,3},{3,4},{4,5},{5,6},{6,7},{7,8},{8,9},{9,10},{10,1... | collective-permute-start | bytes 98312 | tf_op jit(solution)/shard_map/ppermute | solution.py:31
  76.8 8.8 %collective-permute-start.3 = (f32[64,128]{1,0:T(8,128)S(1)}, f32[64,128]{1,0:T(8,128)S(1)}, u32[]{:S(2)}, u32[]{:S(2)}) collective-permute-start(f32[64,128]{1,0:T(8,128)S(1)} %fusion.70), channel_id=1, source_target_pairs={{1,0},{2,1},{3,2},{4,3},{5,4},{6,5},{7,6},{8,7},{9,8},{10,9},{11,1... | collective-permute-start | bytes 98312 | tf_op jit(solution)/shard_map/ppermute | solution.py:31
  93.4 8.8 %collective-permute-start.5 = (f32[64,128]{1,0:T(8,128)S(1)}, f32[64,128]{1,0:T(8,128)S(1)}, u32[]{:S(2)}, u32[]{:S(2)}) collective-permute-start(f32[64,128]{1,0:T(8,128)S(1)} %fusion.69), channel_id=1, source_target_pairs={{1,0},{2,1},{3,2},{4,3},{5,4},{6,5},{7,6},{8,7},{9,8},{10,9},{11,1... | collective-permute-start | bytes 98312 | tf_op jit(solution)/shard_map/ppermute | solution.py:31
  112.8 6.2 %collective-permute-start.10 = (f32[128,128]{1,0:T(8,128)S(1)}, f32[128,128]{1,0:T(8,128)S(1)}, u32[]{:S(2)}, u32[]{:S(2)}) collective-permute-start(f32[128,128]{1,0:T(8,128)S(1)} %get-tuple-element.210), channel_id=1, source_target_pairs={{0,7},{1,0},{2,1},{3,2},{4,3},{5,4},{6,5},{7,6},{8,15},{9,8},{10,9... | collective-permute-start | bytes 196616 | tf_op jit(solution)/shard_map/ppermute | solution.py:23
  114.1 5.8 %collective-permute-start.8 = (f32[128,128]{1,0:T(8,128)S(1)}, f32[128,128]{1,0:T(8,128)S(1)}, u32[]{:S(2)}, u32[]{:S(2)}) collective-permute-start(f32[128,128]{1,0:T(8,128)S(1)} %collective-permute-done.7), channel_id=1, source_target_pairs={{0,1},{1,2},{2,3},{3,4},{4,5},{5,6},{6,7},{7,0},{8,9},{9,10},{10,1... | collective-permute-start | bytes 196616 | tf_op jit(solution)/shard_map/ppermute | solution.py:21
  119.0 6.0 %collective-permute-start.11 = (f32[128,128]{1,0:T(8,128)S(1)}, f32[128,128]{1,0:T(8,128)S(1)}, u32[]{:S(2)}, u32[]{:S(2)}) collective-permute-start(f32[128,128]{1,0:T(8,128)S(1)} %collective-permute-done.10), channel_id=1, source_target_pairs={{0,7},{1,0},{2,1},{3,2},{4,3},{5,4},{6,5},{7,6},{8,15},{9,8},{10,9... | collective-permute-start | bytes 196616 | tf_op jit(solution)/shard_map/ppermute | solution.py:23
  119.9 6.4 %collective-permute-start.9 = (f32[128,128]{1,0:T(8,128)S(1)}, f32[128,128]{1,0:T(8,128)S(1)}, u32[]{:S(2)}, u32[]{:S(2)}) collective-permute-start(f32[128,128]{1,0:T(8,128)S(1)} %collective-permute-done.8), channel_id=1, source_target_pairs={{0,1},{1,2},{2,3},{3,4},{4,5},{5,6},{6,7},{7,0},{8,9},{9,10},{10,1... | collective-permute-start | bytes 196616 | tf_op jit(solution)/shard_map/ppermute | solution.py:21
  137.7 5.9 %collective-permute-start.17 = (f32[128,128]{1,0:T(8,128)S(1)}, f32[128,128]{1,0:T(8,128)S(1)}, u32[]{:S(2)}, u32[]{:S(2)}) collective-permute-start(f32[128,128]{1,0:T(8,128)S(1)} %get-tuple-element.212), channel_id=1, source_target_pairs={{0,7},{1,0},{2,1},{3,2},{4,3},{5,4},{6,5},{7,6},{8,15},{9,8},{10,9... | collective-permute-start | bytes 196616 | tf_op jit(solution)/shard_map/ppermute | solution.py:23
  149.3 5.9 %collective-permute-start.19 = (f32[128,128]{1,0:T(8,128)S(1)}, f32[128,128]{1,0:T(8,128)S(1)}, u32[]{:S(2)}, u32[]{:S(2)}) collective-permute-start(f32[128,128]{1,0:T(8,128)S(1)} %collective-permute-done.18), channel_id=1, source_target_pairs={{0,7},{1,0},{2,1},{3,2},{4,3},{5,4},{6,5},{7,6},{8,15},{9,8},{10,9... | collective-permute-start | bytes 196616 | tf_op jit(solution)/shard_map/ppermute | solution.py:23
  162.0 5.9 %collective-permute-start.24 = (f32[128,128]{1,0:T(8,128)S(1)}, f32[128,128]{1,0:T(8,128)S(1)}, u32[]{:S(2)}, u32[]{:S(2)}) collective-permute-start(f32[128,128]{1,0:T(8,128)S(1)} %get-tuple-element.214), channel_id=1, source_target_pairs={{0,7},{1,0},{2,1},{3,2},{4,3},{5,4},{6,5},{7,6},{8,15},{9,8},{10,9... | collective-permute-start | bytes 196616 | tf_op jit(solution)/shard_map/ppermute | solution.py:23
  167.9 5.9 %collective-permute-start.25 = (f32[128,128]{1,0:T(8,128)S(1)}, f32[128,128]{1,0:T(8,128)S(1)}, u32[]{:S(2)}, u32[]{:S(2)}) collective-permute-start(f32[128,128]{1,0:T(8,128)S(1)} %collective-permute-done.24), channel_id=1, source_target_pairs={{0,7},{1,0},{2,1},{3,2},{4,3},{5,4},{6,5},{7,6},{8,15},{9,8},{10,9... | collective-permute-start | bytes 196616 | tf_op jit(solution)/shard_map/ppermute | solution.py:23
  169.2 5.9 %collective-permute-start.23 = (f32[128,128]{1,0:T(8,128)S(1)}, f32[128,128]{1,0:T(8,128)S(1)}, u32[]{:S(2)}, u32[]{:S(2)}) collective-permute-start(f32[128,128]{1,0:T(8,128)S(1)} %collective-permute-done.22), channel_id=1, source_target_pairs={{0,1},{1,2},{2,3},{3,4},{4,5},{5,6},{6,7},{7,0},{8,9},{9,10},{10,1... | collective-permute-start | bytes 196616 | tf_op jit(solution)/shard_map/ppermute | solution.py:21
  187.8 6.2 %collective-permute-start.29 = (f32[128,128]{1,0:T(8,128)S(1)}, f32[128,128]{1,0:T(8,128)S(1)}, u32[]{:S(2)}, u32[]{:S(2)}) collective-permute-start(f32[128,128]{1,0:T(8,128)S(1)} %collective-permute-done.28), channel_id=1, source_target_pairs={{0,1},{1,2},{2,3},{3,4},{4,5},{5,6},{6,7},{7,0},{8,9},{9,10},{10,1... | collective-permute-start | bytes 196616 | tf_op jit(solution)/shard_map/ppermute | solution.py:21
  192.3 6.6 %collective-permute-start.32 = (f32[128,128]{1,0:T(8,128)S(1)}, f32[128,128]{1,0:T(8,128)S(1)}, u32[]{:S(2)}, u32[]{:S(2)}) collective-permute-start(f32[128,128]{1,0:T(8,128)S(1)} %collective-permute-done.31), channel_id=1, source_target_pairs={{0,7},{1,0},{2,1},{3,2},{4,3},{5,4},{6,5},{7,6},{8,15},{9,8},{10,9... | collective-permute-start | bytes 196616 | tf_op jit(solution)/shard_map/ppermute | solution.py:23
  194.0 6.2 %collective-permute-start.30 = (f32[128,128]{1,0:T(8,128)S(1)}, f32[128,128]{1,0:T(8,128)S(1)}, u32[]{:S(2)}, u32[]{:S(2)}) collective-permute-start(f32[128,128]{1,0:T(8,128)S(1)} %collective-permute-done.29), channel_id=1, source_target_pairs={{0,1},{1,2},{2,3},{3,4},{4,5},{5,6},{6,7},{7,0},{8,9},{9,10},{10,1... | collective-permute-start | bytes 196616 | tf_op jit(solution)/shard_map/ppermute | solution.py:21
  198.9 5.8 %collective-permute-start.33 = (f32[128,128]{1,0:T(8,128)S(1)}, f32[128,128]{1,0:T(8,128)S(1)}, u32[]{:S(2)}, u32[]{:S(2)}) collective-permute-start(f32[128,128]{1,0:T(8,128)S(1)} %collective-permute-done.32), channel_id=1, source_target_pairs={{0,7},{1,0},{2,1},{3,2},{4,3},{5,4},{6,5},{7,6},{8,15},{9,8},{10,9... | collective-permute-start | bytes 196616 | tf_op jit(solution)/shard_map/ppermute | solution.py:23
  211.5 5.9 %collective-permute-start.38 = (f32[128,128]{1,0:T(8,128)S(1)}, f32[128,128]{1,0:T(8,128)S(1)}, u32[]{:S(2)}, u32[]{:S(2)}) collective-permute-start(f32[128,128]{1,0:T(8,128)S(1)} %get-tuple-element.218), channel_id=1, source_target_pairs={{0,7},{1,0},{2,1},{3,2},{4,3},{5,4},{6,5},{7,6},{8,15},{9,8},{10,9... | collective-permute-start | bytes 196616 | tf_op jit(solution)/shard_map/ppermute | solution.py:23
  212.9 5.9 %collective-permute-start.36 = (f32[128,128]{1,0:T(8,128)S(1)}, f32[128,128]{1,0:T(8,128)S(1)}, u32[]{:S(2)}, u32[]{:S(2)}) collective-permute-start(f32[128,128]{1,0:T(8,128)S(1)} %collective-permute-done.35), channel_id=1, source_target_pairs={{0,1},{1,2},{2,3},{3,4},{4,5},{5,6},{6,7},{7,0},{8,9},{9,10},{10,1... | collective-permute-start | bytes 196616 | tf_op jit(solution)/shard_map/ppermute | solution.py:21
  223.3 6.0 %collective-permute-start.40 = (f32[128,128]{1,0:T(8,128)S(1)}, f32[128,128]{1,0:T(8,128)S(1)}, u32[]{:S(2)}, u32[]{:S(2)}) collective-permute-start(f32[128,128]{1,0:T(8,128)S(1)} %collective-permute-done.39), channel_id=1, source_target_pairs={{0,7},{1,0},{2,1},{3,2},{4,3},{5,4},{6,5},{7,6},{8,15},{9,8},{10,9... | collective-permute-start | bytes 196616 | tf_op jit(solution)/shard_map/ppermute | solution.py:23
  232.2 26.5 %collective-permute-start.41 = (f32[64,128]{1,0:T(8,128)S(1)}, f32[64,128]{1,0:T(8,128)S(1)}, u32[]{:S(2)}, u32[]{:S(2)}) collective-permute-start(f32[64,128]{1,0:T(8,128)S(1)} %fusion.82), channel_id=1, source_target_pairs={{0,1},{1,2},{2,3},{3,4},{4,5},{5,6},{6,7},{7,8},{8,9},{9,10},{10,1... | collective-permute-start | bytes 98312 | tf_op jit(solution)/shard_map/ppermute | solution.py:31
  256.8 8.8 %collective-permute-start.42 = (f32[64,128]{1,0:T(8,128)S(1)}, f32[64,128]{1,0:T(8,128)S(1)}, u32[]{:S(2)}, u32[]{:S(2)}) collective-permute-start(f32[64,128]{1,0:T(8,128)S(1)} %fusion.68), channel_id=1, source_target_pairs={{1,0},{2,1},{3,2},{4,3},{5,4},{6,5},{7,6},{8,7},{9,8},{10,9},{11,1... | collective-permute-start | bytes 98312 | tf_op jit(solution)/shard_map/ppermute | solution.py:31
  271.6 8.8 %collective-permute-start.44 = (f32[64,128]{1,0:T(8,128)S(1)}, f32[64,128]{1,0:T(8,128)S(1)}, u32[]{:S(2)}, u32[]{:S(2)}) collective-permute-start(f32[64,128]{1,0:T(8,128)S(1)} %fusion.67), channel_id=1, source_target_pairs={{1,0},{2,1},{3,2},{4,3},{5,4},{6,5},{7,6},{8,7},{9,8},{10,9},{11,1... | collective-permute-start | bytes 98312 | tf_op jit(solution)/shard_map/ppermute | solution.py:31
  286.4 8.8 %collective-permute-start.46 = (f32[64,128]{1,0:T(8,128)S(1)}, f32[64,128]{1,0:T(8,128)S(1)}, u32[]{:S(2)}, u32[]{:S(2)}) collective-permute-start(f32[64,128]{1,0:T(8,128)S(1)} %fusion.66), channel_id=1, source_target_pairs={{1,0},{2,1},{3,2},{4,3},{5,4},{6,5},{7,6},{8,7},{9,8},{10,9},{11,1... | collective-permute-start | bytes 98312 | tf_op jit(solution)/shard_map/ppermute | solution.py:31
  301.2 8.8 %collective-permute-start.48 = (f32[64,128]{1,0:T(8,128)S(1)}, f32[64,128]{1,0:T(8,128)S(1)}, u32[]{:S(2)}, u32[]{:S(2)}) collective-permute-start(f32[64,128]{1,0:T(8,128)S(1)} %fusion.65), channel_id=1, source_target_pairs={{1,0},{2,1},{3,2},{4,3},{5,4},{6,5},{7,6},{8,7},{9,8},{10,9},{11,1... | collective-permute-start | bytes 98312 | tf_op jit(solution)/shard_map/ppermute | solution.py:31
  316.0 8.8 %collective-permute-start.50 = (f32[64,128]{1,0:T(8,128)S(1)}, f32[64,128]{1,0:T(8,128)S(1)}, u32[]{:S(2)}, u32[]{:S(2)}) collective-permute-start(f32[64,128]{1,0:T(8,128)S(1)} %fusion.64), channel_id=1, source_target_pairs={{1,0},{2,1},{3,2},{4,3},{5,4},{6,5},{7,6},{8,7},{9,8},{10,9},{11,1... | collective-permute-start | bytes 98312 | tf_op jit(solution)/shard_map/ppermute | solution.py:31
  330.9 8.8 %collective-permute-start.52 = (f32[64,128]{1,0:T(8,128)S(1)}, f32[64,128]{1,0:T(8,128)S(1)}, u32[]{:S(2)}, u32[]{:S(2)}) collective-permute-start(f32[64,128]{1,0:T(8,128)S(1)} %fusion.63), channel_id=1, source_target_pairs={{1,0},{2,1},{3,2},{4,3},{5,4},{6,5},{7,6},{8,7},{9,8},{10,9},{11,1... | collective-permute-start | bytes 98312 | tf_op jit(solution)/shard_map/ppermute | solution.py:31
  345.7 8.8 %collective-permute-start.54 = (f32[64,128]{1,0:T(8,128)S(1)}, f32[64,128]{1,0:T(8,128)S(1)}, u32[]{:S(2)}, u32[]{:S(2)}) collective-permute-start(f32[64,128]{1,0:T(8,128)S(1)} %fusion.62), channel_id=1, source_target_pairs={{1,0},{2,1},{3,2},{4,3},{5,4},{6,5},{7,6},{8,7},{9,8},{10,9},{11,1... | collective-permute-start | bytes 98312 | tf_op jit(solution)/shard_map/ppermute | solution.py:31
  364.5 6.7 %collective-permute-start.59 = (f32[128,128]{1,0:T(8,128)S(1)}, f32[128,128]{1,0:T(8,128)S(1)}, u32[]{:S(2)}, u32[]{:S(2)}) collective-permute-start(f32[128,128]{1,0:T(8,128)S(1)} %get-tuple-element.220), channel_id=1, source_target_pairs={{0,7},{1,0},{2,1},{3,2},{4,3},{5,4},{6,5},{7,6},{8,15},{9,8},{10,9... | collective-permute-start | bytes 196616 | tf_op jit(solution)/shard_map/ppermute | solution.py:23
  366.4 6.0 %collective-permute-start.57 = (f32[128,128]{1,0:T(8,128)S(1)}, f32[128,128]{1,0:T(8,128)S(1)}, u32[]{:S(2)}, u32[]{:S(2)}) collective-permute-start(f32[128,128]{1,0:T(8,128)S(1)} %collective-permute-done.56), channel_id=1, source_target_pairs={{0,1},{1,2},{2,3},{3,4},{4,5},{5,6},{6,7},{7,0},{8,9},{9,10},{10,1... | collective-permute-start | bytes 196616 | tf_op jit(solution)/shard_map/ppermute | solution.py:21
  377.0 5.8 %collective-permute-start.61 = (f32[128,128]{1,0:T(8,128)S(1)}, f32[128,128]{1,0:T(8,128)S(1)}, u32[]{:S(2)}, u32[]{:S(2)}) collective-permute-start(f32[128,128]{1,0:T(8,128)S(1)} %collective-permute-done.60), channel_id=1, source_target_pairs={{0,7},{1,0},{2,1},{3,2},{4,3},{5,4},{6,5},{7,6},{8,15},{9,8},{10,9... | collective-permute-start | bytes 196616 | tf_op jit(solution)/shard_map/ppermute | solution.py:23
  395.4 5.9 %collective-permute-start.67 = (f32[128,128]{1,0:T(8,128)S(1)}, f32[128,128]{1,0:T(8,128)S(1)}, u32[]{:S(2)}, u32[]{:S(2)}) collective-permute-start(f32[128,128]{1,0:T(8,128)S(1)} %collective-permute-done.66), channel_id=1, source_target_pairs={{0,7},{1,0},{2,1},{3,2},{4,3},{5,4},{6,5},{7,6},{8,15},{9,8},{10,9... | collective-permute-start | bytes 196616 | tf_op jit(solution)/shard_map/ppermute | solution.py:23
  396.7 6.0 %collective-permute-start.65 = (f32[128,128]{1,0:T(8,128)S(1)}, f32[128,128]{1,0:T(8,128)S(1)}, u32[]{:S(2)}, u32[]{:S(2)}) collective-permute-start(f32[128,128]{1,0:T(8,128)S(1)} %collective-permute-done.64), channel_id=1, source_target_pairs={{0,1},{1,2},{2,3},{3,4},{4,5},{5,6},{6,7},{7,0},{8,9},{9,10},{10,1... | collective-permute-start | bytes 196616 | tf_op jit(solution)/shard_map/ppermute | solution.py:21
  401.3 6.8 %collective-permute-start.68 = (f32[128,128]{1,0:T(8,128)S(1)}, f32[128,128]{1,0:T(8,128)S(1)}, u32[]{:S(2)}, u32[]{:S(2)}) collective-permute-start(f32[128,128]{1,0:T(8,128)S(1)} %collective-permute-done.67), channel_id=1, source_target_pairs={{0,7},{1,0},{2,1},{3,2},{4,3},{5,4},{6,5},{7,6},{8,15},{9,8},{10,9... | collective-permute-start | bytes 196616 | tf_op jit(solution)/shard_map/ppermute | solution.py:23
  421.1 5.9 %collective-permute-start.74 = (f32[128,128]{1,0:T(8,128)S(1)}, f32[128,128]{1,0:T(8,128)S(1)}, u32[]{:S(2)}, u32[]{:S(2)}) collective-permute-start(f32[128,128]{1,0:T(8,128)S(1)} %collective-permute-done.73), channel_id=1, source_target_pairs={{0,7},{1,0},{2,1},{3,2},{4,3},{5,4},{6,5},{7,6},{8,15},{9,8},{10,9... | collective-permute-start | bytes 196616 | tf_op jit(solution)/shard_map/ppermute | solution.py:23
  422.4 5.9 %collective-permute-start.72 = (f32[128,128]{1,0:T(8,128)S(1)}, f32[128,128]{1,0:T(8,128)S(1)}, u32[]{:S(2)}, u32[]{:S(2)}) collective-permute-start(f32[128,128]{1,0:T(8,128)S(1)} %collective-permute-done.71), channel_id=1, source_target_pairs={{0,1},{1,2},{2,3},{3,4},{4,5},{5,6},{6,7},{7,0},{8,9},{9,10},{10,1... | collective-permute-start | bytes 196616 | tf_op jit(solution)/shard_map/ppermute | solution.py:21
  441.0 6.3 %collective-permute-start.78 = (f32[128,128]{1,0:T(8,128)S(1)}, f32[128,128]{1,0:T(8,128)S(1)}, u32[]{:S(2)}, u32[]{:S(2)}) collective-permute-start(f32[128,128]{1,0:T(8,128)S(1)} %collective-permute-done.77), channel_id=1, source_target_pairs={{0,1},{1,2},{2,3},{3,4},{4,5},{5,6},{6,7},{7,0},{8,9},{9,10},{10,1... | collective-permute-start | bytes 196616 | tf_op jit(solution)/shard_map/ppermute | solution.py:21
  445.5 6.8 %collective-permute-start.81 = (f32[128,128]{1,0:T(8,128)S(1)}, f32[128,128]{1,0:T(8,128)S(1)}, u32[]{:S(2)}, u32[]{:S(2)}) collective-permute-start(f32[128,128]{1,0:T(8,128)S(1)} %collective-permute-done.80), channel_id=1, source_target_pairs={{0,7},{1,0},{2,1},{3,2},{4,3},{5,4},{6,5},{7,6},{8,15},{9,8},{10,9... | collective-permute-start | bytes 196616 | tf_op jit(solution)/shard_map/ppermute | solution.py:23
  447.3 6.2 %collective-permute-start.79 = (f32[128,128]{1,0:T(8,128)S(1)}, f32[128,128]{1,0:T(8,128)S(1)}, u32[]{:S(2)}, u32[]{:S(2)}) collective-permute-start(f32[128,128]{1,0:T(8,128)S(1)} %collective-permute-done.78), channel_id=1, source_target_pairs={{0,1},{1,2},{2,3},{3,4},{4,5},{5,6},{6,7},{7,0},{8,9},{9,10},{10,1... | collective-permute-start | bytes 196616 | tf_op jit(solution)/shard_map/ppermute | solution.py:21
  452.2 5.8 %collective-permute-start.82 = (f32[128,128]{1,0:T(8,128)S(1)}, f32[128,128]{1,0:T(8,128)S(1)}, u32[]{:S(2)}, u32[]{:S(2)}) collective-permute-start(f32[128,128]{1,0:T(8,128)S(1)} %collective-permute-done.81), channel_id=1, source_target_pairs={{0,7},{1,0},{2,1},{3,2},{4,3},{5,4},{6,5},{7,6},{8,15},{9,8},{10,9... | collective-permute-start | bytes 196616 | tf_op jit(solution)/shard_map/ppermute | solution.py:23
  470.7 5.8 %collective-permute-start.88 = (f32[128,128]{1,0:T(8,128)S(1)}, f32[128,128]{1,0:T(8,128)S(1)}, u32[]{:S(2)}, u32[]{:S(2)}) collective-permute-start(f32[128,128]{1,0:T(8,128)S(1)} %collective-permute-done.87), channel_id=1, source_target_pairs={{0,7},{1,0},{2,1},{3,2},{4,3},{5,4},{6,5},{7,6},{8,15},{9,8},{10,9... | collective-permute-start | bytes 196616 | tf_op jit(solution)/shard_map/ppermute | solution.py:23
  476.6 6.0 %collective-permute-start.89 = (f32[128,128]{1,0:T(8,128)S(1)}, f32[128,128]{1,0:T(8,128)S(1)}, u32[]{:S(2)}, u32[]{:S(2)}) collective-permute-start(f32[128,128]{1,0:T(8,128)S(1)} %collective-permute-done.88), channel_id=1, source_target_pairs={{0,7},{1,0},{2,1},{3,2},{4,3},{5,4},{6,5},{7,6},{8,15},{9,8},{10,9... | collective-permute-start | bytes 196616 | tf_op jit(solution)/shard_map/ppermute | solution.py:23
  485.6 25.2 %collective-permute-start.90 = (f32[64,128]{1,0:T(8,128)S(1)}, f32[64,128]{1,0:T(8,128)S(1)}, u32[]{:S(2)}, u32[]{:S(2)}) collective-permute-start(f32[64,128]{1,0:T(8,128)S(1)} %fusion.75), channel_id=1, source_target_pairs={{0,1},{1,2},{2,3},{3,4},{4,5},{5,6},{6,7},{7,8},{8,9},{9,10},{10,1... | collective-permute-start | bytes 98312 | tf_op jit(solution)/shard_map/ppermute | solution.py:31
  508.8 8.8 %collective-permute-start.91 = (f32[64,128]{1,0:T(8,128)S(1)}, f32[64,128]{1,0:T(8,128)S(1)}, u32[]{:S(2)}, u32[]{:S(2)}) collective-permute-start(f32[64,128]{1,0:T(8,128)S(1)} %fusion.61), channel_id=1, source_target_pairs={{1,0},{2,1},{3,2},{4,3},{5,4},{6,5},{7,6},{8,7},{9,8},{10,9},{11,1... | collective-permute-start | bytes 98312 | tf_op jit(solution)/shard_map/ppermute | solution.py:31
  523.6 8.8 %collective-permute-start.93 = (f32[64,128]{1,0:T(8,128)S(1)}, f32[64,128]{1,0:T(8,128)S(1)}, u32[]{:S(2)}, u32[]{:S(2)}) collective-permute-start(f32[64,128]{1,0:T(8,128)S(1)} %fusion.60), channel_id=1, source_target_pairs={{1,0},{2,1},{3,2},{4,3},{5,4},{6,5},{7,6},{8,7},{9,8},{10,9},{11,1... | collective-permute-start | bytes 98312 | tf_op jit(solution)/shard_map/ppermute | solution.py:31
  538.5 8.8 %collective-permute-start.95 = (f32[64,128]{1,0:T(8,128)S(1)}, f32[64,128]{1,0:T(8,128)S(1)}, u32[]{:S(2)}, u32[]{:S(2)}) collective-permute-start(f32[64,128]{1,0:T(8,128)S(1)} %fusion.59), channel_id=1, source_target_pairs={{1,0},{2,1},{3,2},{4,3},{5,4},{6,5},{7,6},{8,7},{9,8},{10,9},{11,1... | collective-permute-start | bytes 98312 | tf_op jit(solution)/shard_map/ppermute | solution.py:31
  555.0 8.8 %collective-permute-start.97 = (f32[64,128]{1,0:T(8,128)S(1)}, f32[64,128]{1,0:T(8,128)S(1)}, u32[]{:S(2)}, u32[]{:S(2)}) collective-permute-start(f32[64,128]{1,0:T(8,128)S(1)} %fusion.58), channel_id=1, source_target_pairs={{1,0},{2,1},{3,2},{4,3},{5,4},{6,5},{7,6},{8,7},{9,8},{10,9},{11,1... | collective-permute-start | bytes 98312 | tf_op jit(solution)/shard_map/ppermute | solution.py:31
  (66 other events, 383.6 us)
